TPU v7x, 512 devices: a whole 4x8x8 slice. The times are simulated.
512 devices in a mesh: dp: 8 (over y), feat: 64 (over x, z, core).
Axes of the slice: x: 4, y: 8, z: 8, core: 2. Of those that a mesh axis runs over, the one named last changes fastest.
Arguments:
- features: bfloat16 [8, 16384, 128], P('dp', None, 'feat'), may hold values from -6 to 6
- tile_weights: bfloat16 [8, 1536, 128, 128], P('dp', 'feat'), may hold values from -0.15625 to 0.15625
- tile_rows: int32 [8, 1536], P('dp', 'feat'), may hold values from 0 to 1
- tile_owners: int32 [8, 1536, 1], P('dp', 'feat'), may hold values from 0 to 63; in each aligned block of 24 rows (0 to 23, 24 to 47, ..., all dimensions but the last counted through in order) at most 2 rows name the same one
- tile_blocks: int32 [8, 1536], P('dp', 'feat'), may hold values from 0 to 1
- tile_counts: int32 [8, 64], P('dp', 'feat'), may hold values from 6 to 24, as said below
- cotangent: bfloat16 [8, 16384, 1024], P('dp', 'feat'), may hold values from -0.046875 to 0.046875
- w_self: bfloat16 [128, 1024], replicated, may hold values from -0.5 to 0.5
- w_neigh: bfloat16 [128, 1024], replicated, may hold values from -0.5 to 0.5
- bias: float32 [1024], replicated, may hold values from -4 to 4
Outputs:
- grad_self: float32 [128, 1024], P(None, 'feat')
- grad_neigh: float32 [128, 1024], P(None, 'feat')
- grad_bias: float32 [1024], P('feat')
Inputs may be any that keep to these rules, and one draw needn't show every extreme that they name: `tile_owners`: among the 24 tile slots of one device at most 2 name one owner, a bound that some block of them reaches. `tile_counts`: in every batch some device has all 24 slots live.
All inputs are finite; a program needn't handle non-finite values.
Results may differ from a plain program's by a relative error of at most 0.008.
Values may be sent and summed in bfloat16 or wider, within the bound.
No kernel may reach another device: no remote copies, remote signals or barrier semaphores. Data moves between devices by JAX's collectives and lax.ppermute only.
A program may use at most 64 MiB of HBM per device.

v0:
```python
import jax
import jax.numpy as jnp
from jax import lax
from jax.sharding import PartitionSpec as P


def silu_slope(pre_act):
    sigmoid_z = jax.nn.sigmoid(pre_act)
    return sigmoid_z * (1.0 + pre_act * (1.0 - sigmoid_z))


def local(
    features,
    tile_weights,
    tile_rows,
    tile_owners,
    tile_blocks,
    tile_counts,
    cotangent,
    w_self,
    w_neigh,
    bias,
):
    owned = lax.all_to_all(features, "feat", split_axis=1, concat_axis=2, tiled=True)[0]
    node_rows, feat_width = owned.shape
    slot_count = tile_weights.shape[1]
    tile_side = tile_weights.shape[2]
    row_blocks = node_rows // tile_side
    peer_count = lax.axis_size("feat")
    row_index = tile_rows[0]
    owner_index = tile_owners[0, :, 0]
    block_index = tile_blocks[0]
    live = jnp.arange(slot_count, dtype=jnp.int32) < tile_counts[0, 0]
    whole = lax.all_gather(owned, "feat", axis=0, tiled=True)
    picked = whole.reshape(-1, tile_side, feat_width)[owner_index * row_blocks + block_index]
    products = jnp.einsum(
        "kij,kjf->kif", tile_weights[0], picked, preferred_element_type=jnp.float32
    )
    select = (
        (row_index[None, :] == jnp.arange(row_blocks, dtype=jnp.int32)[:, None]) & live[None, :]
    ).astype(jnp.float32)
    summed = jnp.einsum("rk,kif->rif", select, products, precision=lax.Precision.HIGHEST)
    neighbour = summed.reshape(node_rows, feat_width).astype(jnp.bfloat16)
    pre_act = (
        jnp.dot(owned, w_self, preferred_element_type=jnp.float32)
        + jnp.dot(neighbour, w_neigh, preferred_element_type=jnp.float32)
        + bias
    )
    slope = (cotangent[0].astype(jnp.float32) * silu_slope(pre_act)).astype(jnp.bfloat16)
    grad_s = jnp.einsum("nf,nh->fh", owned, slope, preferred_element_type=jnp.float32)
    grad_n = jnp.einsum("nf,nh->fh", neighbour, slope, preferred_element_type=jnp.float32)
    grad_b = jnp.sum(slope.astype(jnp.float32), axis=0)
    total_s, total_n, total_b = lax.psum((grad_s, grad_n, grad_b), ("dp", "feat"))
    column_count = w_self.shape[1] // peer_count
    start = lax.axis_index("feat") * column_count
    out_s = lax.dynamic_slice_in_dim(total_s, start, column_count, 1)
    out_n = lax.dynamic_slice_in_dim(total_n, start, column_count, 1)
    out_b = lax.dynamic_slice_in_dim(total_b, start, column_count, 0)
    return (out_s, out_n, out_b)


def solution(mesh):
    return jax.shard_map(
        local,
        mesh=mesh,
        in_specs=(
            P("dp", None, "feat"),
            P("dp", "feat", None, None),
            P("dp", "feat"),
            P("dp", "feat", None),
            P("dp", "feat"),
            P("dp", "feat"),
            P("dp", "feat", None),
            P(),
            P(),
            P(),
        ),
        out_specs=(P(None, "feat"), P(None, "feat"), P("feat")),
        check_vma=False,
    )
```

profile of v0, /device:TPU:23, one launch (start us, length us, event | category | flops | bytes accessed | tf_op | source)
XLA Modules:
  0.0 554.2 jit_solution(6314317441695136422)
XLA Ops:
  7.2 15.4 %copy.26 = bf16[1,16384,2]{2,0,1:T(2,128)(2,1)} copy(bf16[1,16384,2]{1,2,0:T(2,128)(2,1)} %param.10) | data formatting | bytes 131072 | tf_op args[0]
  22.6 0.5 broadcast.52
  23.1 90.8 %reduce = bf16[16384,2]{1,0:T(8,128)(2,1)} reduce(bf16[16384,1,2]{2,1,0:T(2,128)(2,1)} %bitcast.51, bf16[]{:T(256)} %broadcast.52), dimensions={1}, to_apply=%bitcast.36.reduce_sub_computation | reduce | bytes 131074
  113.9 7.1 %reshape.61 = bf16[64,2,256]{2,1,0:T(2,128)(2,1)S(1)} reshape(bf16[16384,2]{1,0:T(8,128)(2,1)} %reduce) | data formatting | bytes 131072
  121.0 21.9 %all_to_all.15 = bf16[64,2,256]{2,1,0:T(2,128)(2,1)S(1)} all-to-all(bf16[64,2,256]{2,1,0:T(2,128)(2,1)S(1)} %reshape.61), channel_id=1, replica_groups=mesh['dp'=8,'feat'=64] {'feat'}, dimensions={0} | all-to-all | bytes 131072 | tf_op jit(solution)/shard_map/all_to_all | solution.py:24
  142.9 16.4 %reshape.62 = bf16[16384,1,2]{2,1,0:T(2,128)(2,1)} reshape(bf16[64,2,256]{2,1,0:T(2,128)(2,1)S(1)} %all_to_all.15) | data formatting | bytes 131072
  159.3 15.4 %copy.27 = bf16[1,16384,2]{1,2,0:T(2,128)(2,1)S(1)} copy(bf16[1,16384,2]{2,0,1:T(2,128)(2,1)} %bitcast.52) | data formatting | bytes 131072 | tf_op jit(solution)/shard_map/all_to_all | solution.py:24
  174.7 0.1 copy.28
  174.8 0.7 squeeze.14
  175.5 0.2 all-reduce.3.cloned.1.call-start
  176.4 1.2 fusion.10
  177.6 77.5 %all-gather.2.cloned.1.call-done = bf16[16384,128]{0,1:T(8,128)(2,1)} async-done(((bf16[256,128]{0,1:T(8,128)(2,1)}), bf16[16384,128]{0,1:T(8,128)(2,1)}) %all-gather.2.cloned.1.call-update) | async-done | bytes 4194320 | tf_op jit(solution)/shard_map/all_gather | solution.py:34
  255.0 6.4 %copy.29 = bf16[16384,128]{1,0:T(8,128)(2,1)} copy(bf16[16384,128]{0,1:T(8,128)(2,1)} %all-gather.2.cloned.1.call-done) | data formatting | bytes 8388608 | tf_op jit(solution)/shard_map/all_gather | solution.py:34
  261.4 2.9 gather_fusion
  264.4 1.9 convolution_bitcast_fusion
  266.2 2.0 copy.31
  268.2 0.6 convolution_convert_fusion
  268.9 1.8 convert_reduce_fusion
  270.6 1.1 fusion.11
  271.8 1.1 convolution_bitcast_fusion.1
  272.9 96.3 %psum.23 = f32[1024]{0:T(1024)S(1)} all-reduce(f32[1024]{0:T(1024)S(1)} %get-tuple-element.5), channel_id=1, replica_groups=mesh['dp'=8,'feat'=64] {'dp','feat'}, use_global_device_ids=true, to_apply=%region_3.0 | all-reduce | flops 1024 | bytes 8192 | tf_op jit(solution)/shard_map/psum | solution.py:53
  369.3 0.6 dynamic_slice.11
  369.9 176.2 %all-reduce.3.cloned.1.call-done = (f32[128,1024]{0,1:T(8,128)}, f32[128,1024]{0,1:T(8,128)}) async-done(((f32[128,1024]{0,1:T(8,128)}, f32[128,1024]{0,1:T(8,128)}), (f32[128,1024]{0,1:T(8,128)}, f32[128,1024]{0,1:T(8,128)})) %all-reduce.3.cloned.1.call-update) | async-done | bytes 1048592 | tf_op jit(solution)/shard_map/psum | solution.py:53
  546.0 1.3 constant_dynamic-slice_fusion
  (22 shorter events, 0.1 us)
Async XLA Ops:
  7.2 257.2 %copy-start = (bf16[1,24,128,128]{3,2,1,0:T(8,128)(2,1)S(1)}, bf16[1,24,128,128]{3,2,1,0:T(8,128)(2,1)}, u32[]{:S(2)}) copy-start(bf16[1,24,128,128]{3,2,1,0:T(8,128)(2,1)} %param.11) | copy-start | bytes 2359300
  7.2 247.8 %all-gather.2.cloned.1.call-start = ((), (), s32[]{:S(2)}) async-start(), calls=%async_computation.1 | async-start | bytes 4259840 | tf_op jit(solution)/shard_map/all_gather | solution.py:34
  159.3 17.1 %copy-start.5 = (s32[1,24]{1,0:T(1,128)S(1)}, s32[1,24]{1,0:T(1,128)}, u32[]{:S(2)}) copy-start(s32[1,24]{1,0:T(1,128)} %param.14) | copy-start | bytes 292
  159.3 17.1 %copy-start.6 = (s32[1,24,1]{1,2,0:T(1,128)S(1)}, s32[1,24,1]{1,2,0:T(1,128)}, u32[]{:S(2)}) copy-start(s32[1,24,1]{1,2,0:T(1,128)} %param.13) | copy-start | bytes 292
  159.3 17.1 %copy-start.2 = (bf16[128,1024]{1,0:T(8,128)(2,1)S(1)}, bf16[128,1024]{1,0:T(8,128)(2,1)}, u32[]{:S(2)}) copy-start(bf16[128,1024]{1,0:T(8,128)(2,1)} %param.17) | copy-start | bytes 786436
  175.5 370.6 %all-reduce.3.cloned.1.call-start = ((), (), s32[]{:S(2)}) async-start(), calls=%async_computation.2 | async-start | bytes 2097152 | tf_op jit(solution)/shard_map/psum | solution.py:53
  261.4 6.8 %copy-start.3 = (s32[1,24]{1,0:T(1,128)S(1)}, s32[1,24]{1,0:T(1,128)}, u32[]{:S(2)}) copy-start(s32[1,24]{1,0:T(1,128)} %param.12) | copy-start | bytes 292
  264.4 4.5 copy-start.4
  268.8 3.0 copy-start.1
Sparse Core Ops, SparseCore 0:
  175.6 79.3 all-gather.1
  273.1 272.9 all-reduce.2
where the time goes:
time: 556 us; the launch traced here: 554 us
  waiting for transfers between devices  254 us (46%)
  blocking collectives  118 us (21%)
  other arithmetic  90.8 us (16%)
  local copies, waits for them, and re-layouts  68.7 us (12%)
  between operations  14.9 us (3%)
  matrix products  7.67 us (1%)
    psum x1, waiting for transfers between devices, local(): lax.psum((grad_s, grad_n, grad_b), ('dp', 'feat'))  176 us
    psum x1, blocking collectives, local(): lax.psum((grad_s, grad_n, grad_b), ('dp', 'feat'))  96.3 us
    unnamed x1, other arithmetic  90.8 us
    all_gather x1, waiting for transfers between devices, local(): whole = lax.all_gather(owned, 'feat', axis=0, tiled=True)  77.5 us
    unnamed x19, local copies, waits for them, and re-layouts  39.5 us
    all_to_all x1, blocking collectives, local(): lax.all_to_all(features, 'feat', split_axis=1, concat_axis=2, tiled=True)[0]  21.9 us
    all_to_all x2, local copies, waits for them, and re-layouts, local(): lax.all_to_all(features, 'feat', split_axis=1, concat_axis=2, tiled=True)[0]  15.5 us
  transfers between devices with their start and end apart: 2, of which 2 were waited for; matrix products, arithmetic and copies ran while one was open for 0% of the time, Pallas kernels for 0%

commit v1 on v0

--- a/solution.py
+++ b/solution.py
@@ -31,7 +31,9 @@
     owner_index = tile_owners[0, :, 0]
     block_index = tile_blocks[0]
     live = jnp.arange(slot_count, dtype=jnp.int32) < tile_counts[0, 0]
-    whole = lax.all_gather(owned, "feat", axis=0, tiled=True)
+    whole = jnp.concatenate(
+        lax.all_to_all(jnp.stack([owned] * lax.axis_size("feat")), "feat", 0, 0), axis=0
+    )
     picked = whole.reshape(-1, tile_side, feat_width)[owner_index * row_blocks + block_index]
     products = jnp.einsum(
         "kij,kjf->kif", tile_weights[0], picked, preferred_element_type=jnp.float32

time: 556 us -> 573 us (1.031)
  waiting for transfers between devices: 254 us -> 269 us
  starting transfers between devices: 0.26 us -> 7.93 us
    all_to_all x0 -> x1, waiting for transfers between devices: none -> 94.5 us  [local(): lax.all_to_all(jnp.stack([owned] * lax.axis_size('feat')), 'feat', 0, 0)]
    all_gather x1 -> x0, waiting for transfers between devices: 77.5 us -> none  [local(): whole = lax.all_gather(owned, 'feat', axis=0, tiled=True)]
    all_to_all x0 -> x1, starting transfers between devices: none -> 7.71 us  [local(): lax.all_to_all(jnp.stack([owned] * lax.axis_size('feat')), 'feat', 0, 0)]
    all_gather x1 -> x0, local copies, waits for them, and re-layouts: 6.42 us -> none  [local(): whole = lax.all_gather(owned, 'feat', axis=0, tiled=True)]
    unnamed x19 -> x17, local copies, waits for them, and re-layouts: 39.5 us -> 39.6 us
where the time goes in v1:
time: 573 us; the launch traced here: 572 us
  waiting for transfers between devices  269 us (47%)
  blocking collectives  117 us (20%)
  other arithmetic  90.8 us (16%)
  local copies, waits for them, and re-layouts  64.9 us (11%)
  between operations  14.9 us (3%)
  starting transfers between devices  7.93 us (1%)
  matrix products  6.86 us (1%)
    psum x1, waiting for transfers between devices, local(): lax.psum((grad_s, grad_n, grad_b), ('dp', 'feat'))  174 us
    psum x1, blocking collectives, local(): lax.psum((grad_s, grad_n, grad_b), ('dp', 'feat'))  95.6 us
    all_to_all x1, waiting for transfers between devices, local(): lax.all_to_all(jnp.stack([owned] * lax.axis_size('feat')), 'feat', 0, 0)  94.5 us
    unnamed x1, other arithmetic  90.7 us
    unnamed x17, local copies, waits for them, and re-layouts  39.6 us
    all_to_all x1, blocking collectives, local(): lax.all_to_all(features, 'feat', split_axis=1, concat_axis=2, tiled=True)[0]  21.9 us
    all_to_all x2, local copies, waits for them, and re-layouts, local(): lax.all_to_all(features, 'feat', split_axis=1, concat_axis=2, tiled=True)[0]  15.4 us
  transfers between devices with their start and end apart: 2, of which 2 were waited for; matrix products, arithmetic and copies ran while one was open for 0% of the time, Pallas kernels for 0%

profile of v1, /device:TPU:23, one launch (start us, length us, event | category | flops | bytes accessed | tf_op | source)
XLA Modules:
  0.0 571.7 jit_solution(8708013582282710568)
XLA Ops:
  7.2 15.4 %copy.21 = bf16[1,16384,2]{2,0,1:T(2,128)(2,1)} copy(bf16[1,16384,2]{1,2,0:T(2,128)(2,1)} %param.10) | data formatting | bytes 131072 | tf_op args[0]
  22.6 0.5 broadcast.53
  23.1 90.7 %reduce = bf16[16384,2]{1,0:T(8,128)(2,1)} reduce(bf16[16384,1,2]{2,1,0:T(2,128)(2,1)} %bitcast.51, bf16[]{:T(256)} %broadcast.53), dimensions={1}, to_apply=%bitcast.36.reduce_sub_computation | reduce | bytes 131074
  113.8 7.1 %reshape.59 = bf16[64,2,256]{2,1,0:T(2,128)(2,1)S(1)} reshape(bf16[16384,2]{1,0:T(8,128)(2,1)} %reduce) | data formatting | bytes 131072
  121.0 21.9 %all_to_all.20 = bf16[64,2,256]{2,1,0:T(2,128)(2,1)S(1)} all-to-all(bf16[64,2,256]{2,1,0:T(2,128)(2,1)S(1)} %reshape.59), channel_id=1, replica_groups=mesh['dp'=8,'feat'=64] {'feat'}, dimensions={0} | all-to-all | bytes 131072 | tf_op jit(solution)/shard_map/all_to_all | solution.py:24
  142.8 16.5 %reshape.60 = bf16[16384,1,2]{2,1,0:T(2,128)(2,1)} reshape(bf16[64,2,256]{2,1,0:T(2,128)(2,1)S(1)} %all_to_all.20) | data formatting | bytes 131072
  159.3 15.3 %copy.22 = bf16[1,16384,2]{1,2,0:T(2,128)(2,1)S(1)} copy(bf16[1,16384,2]{2,0,1:T(2,128)(2,1)} %bitcast.52) | data formatting | bytes 131072 | tf_op jit(solution)/shard_map/all_to_all | solution.py:24
  174.8 0.1 copy.24
  174.9 3.0 stack.3
  177.9 7.7 %all-to-all-start.1 = ((bf16[64,256,128]{2,1,0:T(8,128)(2,1)}), bf16[64,256,128]{2,1,0:T(8,128)(2,1)}, u32[]{:S(2)}, u32[]{:S(2)}) async-start(bf16[64,256,128]{2,1,0:T(8,128)(2,1)} %stack.3), calls=%async_computation.1 | async-start | bytes 8388608 | tf_op jit(solution)/shard_map/all_to_all | solution.py:35
  185.6 0.2 all-reduce.3.cloned.1.call-start
  186.6 0.3 fusion.10
  186.9 94.5 %all-to-all-done.1 = bf16[64,256,128]{2,1,0:T(8,128)(2,1)} async-done(((bf16[64,256,128]{2,1,0:T(8,128)(2,1)}), bf16[64,256,128]{2,1,0:T(8,128)(2,1)}, u32[]{:S(2)}, u32[]{:S(2)}) %all-to-all-start.1) | async-done | bytes 4194336 | tf_op jit(solution)/shard_map/all_to_all | solution.py:35
  281.4 2.9 gather_fusion
  284.3 1.9 convolution_bitcast_fusion
  286.2 2.0 copy.26
  288.1 0.6 convolution_convert_fusion
  288.8 1.8 convert_reduce_fusion
  290.5 1.1 fusion.11
  291.7 1.2 convolution_bitcast_fusion.1
  292.9 95.6 %psum.23 = f32[1024]{0:T(1024)S(1)} all-reduce(f32[1024]{0:T(1024)S(1)} %get-tuple-element.5), channel_id=1, replica_groups=mesh['dp'=8,'feat'=64] {'dp','feat'}, use_global_device_ids=true, to_apply=%region_3.0 | all-reduce | flops 1024 | bytes 8192 | tf_op jit(solution)/shard_map/psum | solution.py:55
  388.5 0.6 dynamic_slice.11
  389.1 174.4 %all-reduce.3.cloned.1.call-done = (f32[128,1024]{0,1:T(8,128)}, f32[128,1024]{0,1:T(8,128)}) async-done(((f32[128,1024]{0,1:T(8,128)}, f32[128,1024]{0,1:T(8,128)}), (f32[128,1024]{0,1:T(8,128)}, f32[128,1024]{0,1:T(8,128)})) %all-reduce.3.cloned.1.call-update) | async-done | bytes 1048592 | tf_op jit(solution)/shard_map/psum | solution.py:55
  563.5 1.3 constant_dynamic-slice_fusion
  (20 shorter events, 0.2 us)
Async XLA Ops:
  7.2 277.1 %copy-start = (bf16[1,24,128,128]{3,2,1,0:T(8,128)(2,1)S(1)}, bf16[1,24,128,128]{3,2,1,0:T(8,128)(2,1)}, u32[]{:S(2)}) copy-start(bf16[1,24,128,128]{3,2,1,0:T(8,128)(2,1)} %param.11) | copy-start | bytes 2359300
  177.9 8.6 %copy-start.4 = (s32[1,24]{1,0:T(1,128)S(1)}, s32[1,24]{1,0:T(1,128)}, u32[]{:S(2)}) copy-start(s32[1,24]{1,0:T(1,128)} %param.14) | copy-start | bytes 292
  177.9 8.6 %copy-start.5 = (s32[1,24,1]{1,2,0:T(1,128)S(1)}, s32[1,24,1]{1,2,0:T(1,128)}, u32[]{:S(2)}) copy-start(s32[1,24,1]{1,2,0:T(1,128)} %param.13) | copy-start | bytes 292
  177.9 8.7 %copy-start.1 = (bf16[128,1024]{1,0:T(8,128)(2,1)S(1)}, bf16[128,1024]{1,0:T(8,128)(2,1)}, u32[]{:S(2)}) copy-start(bf16[128,1024]{1,0:T(8,128)(2,1)} %param.17) | copy-start | bytes 786436
  177.9 103.5 %all-to-all-start.1 = ((bf16[64,256,128]{2,1,0:T(8,128)(2,1)}), bf16[64,256,128]{2,1,0:T(8,128)(2,1)}, u32[]{:S(2)}, u32[]{:S(2)}) async-start(bf16[64,256,128]{2,1,0:T(8,128)(2,1)} %stack.3), calls=%async_computation.1 | async-start | bytes 8388608 | tf_op jit(solution)/shard_map/all_to_all | solution.py:35
  185.6 377.8 %all-reduce.3.cloned.1.call-start = ((), (), s32[]{:S(2)}) async-start(), calls=%async_computation.2 | async-start | bytes 2097152 | tf_op jit(solution)/shard_map/psum | solution.py:55
  186.9 101.2 %copy-start.2 = (s32[1,24]{1,0:T(1,128)S(1)}, s32[1,24]{1,0:T(1,128)}, u32[]{:S(2)}) copy-start(s32[1,24]{1,0:T(1,128)} %param.12) | copy-start | bytes 292
  284.3 4.5 copy-start.3
Sparse Core Ops, SparseCore 0:
  293.0 270.4 all-reduce.2
